TPU v7x, 32 devices: a whole 2x2x4 slice. The times are simulated.
32 devices in a mesh: grp: 2 (over x), row: 16 (over z, y, core).
Axes of the slice: x: 2, y: 2, z: 4, core: 2. Of those that a mesh axis runs over, the one named last changes fastest.
Arguments:
- sources: bfloat16 [32, 8, 8, 1024], P(('grp', 'row')), parts along dimension 0, may hold values from -6 to 6
- far_left: bfloat16 [64, 15, 48, 1024], P(('grp', 'row')), parts along dimension 0, may hold values from -0.1875 to 0.1875
- far_right: bfloat16 [64, 15, 48, 1024], P(('grp', 'row')), parts along dimension 0, may hold values from -0.078125 to 0.078125
- ranks: int32 [64, 15], P(('grp', 'row')), parts along dimension 0, may hold values from 16 to 48
- near_blocks: bfloat16 [6, 1024, 1024], P('grp'), parts along dimension 0, may hold values from -0.1875 to 0.1875
- near_offsets: int32 [6, 2], P('grp'), parts along dimension 0, may hold values from -1 to 1, as said below
Outputs:
- fields: float32 [32, 8, 8, 1024], P(('grp', 'row')), parts along dimension 0
There are 2 independent parts, one for each index of `grp`. A program takes and returns all parts, laid end to end along the dimension named above; each array names one. Nothing has to cross between parts.
Inputs may be any that keep to these rules, and one draw needn't show every extreme that they name: `near_offsets`: the rows are 3 distinct offsets (a, b); row 0 is the self offset (0, 0).
All inputs are finite; a program needn't handle non-finite values.
Results may differ from a plain program's by a relative error of at most 0.0014.
Values may be sent and summed in bfloat16 or wider, within the bound.
A program may use at most 64 MiB of HBM per device.

v0:
```python
import jax
import jax.numpy as jnp
from jax import lax
from jax.sharding import PartitionSpec as P

RANK = 48
ECOL = 8
SLOTS = 15


def from_behind(value, axis, by):
    count = lax.axis_size(axis)
    return lax.ppermute(value, axis, [(i, (i + by) % count) for i in range(count)])


def padded_2(block, sides, width):
    for axis, dim in sides:
        count = lax.axis_size(axis)
        forward = [(i, i + 1) for i in range(count - 1)]
        backward = [(target, source) for source, target in forward]
        low = lax.ppermute(
            lax.slice_in_dim(block, block.shape[dim] - width, None, axis=dim), axis, forward
        )
        high = lax.ppermute(lax.slice_in_dim(block, 0, width, axis=dim), axis, backward)
        block = jnp.concatenate([low, block, high], axis=dim)
    return block


def slot_mask(rank_row, row_offset, near_offsets):
    col_offset = jnp.arange(SLOTS, dtype=jnp.int32) - (ECOL - 1)
    hit = jnp.any(
        (near_offsets[:, 0][:, None] == row_offset)
        & (near_offsets[:, 1][:, None] == col_offset[None, :]),
        axis=0,
    )
    live = jnp.arange(RANK, dtype=jnp.int32)[None, :] < rank_row[:, None]
    return (live & jnp.logical_not(hit)[:, None]).astype(jnp.float32)


def spread(coeffs):
    padded = jnp.pad(coeffs, ((ECOL, ECOL), (0, 0), (0, 0), (0, 0)))
    columns = [padded[2 * ECOL - 1 - k : 3 * ECOL - 1 - k, k, :, :] for k in range(SLOTS)]
    return jnp.stack(columns, axis=1)


def far_term(source_row, left, right, keep):
    coeffs = jnp.einsum("sbn,krn->skbr", source_row, left, preferred_element_type=jnp.float32)
    coeffs = (coeffs * keep[None, :, None, :]).astype(jnp.bfloat16)
    return jnp.einsum("jkbr,krn->jbn", spread(coeffs), right, preferred_element_type=jnp.float32)


def local(sources, far_left, far_right, ranks, near_blocks, near_offsets):
    cycle_size = lax.axis_size("row")
    place = lax.axis_index("row")
    keep_all = jnp.stack(
        [slot_mask(ranks[w], place - cycle_size * w, near_offsets) for w in range(2)], axis=0
    )
    ecol, beams, width = (sources.shape[1], sources.shape[2], sources.shape[3])

    def source_term(source_row, source_index):
        wrap_bit = (source_index + place >= cycle_size).astype(jnp.int32)
        left = lax.dynamic_index_in_dim(far_left, wrap_bit, 0, keepdims=False)
        right = lax.dynamic_index_in_dim(far_right, wrap_bit, 0, keepdims=False)
        keep = lax.dynamic_index_in_dim(keep_all, wrap_bit, 0, keepdims=False)
        return far_term(source_row, left, right, keep)

    gathered = lax.all_gather(sources, "row", axis=0, tiled=True)

    def step(source_index, accums):
        down_acc, up_acc = accums
        source_row = lax.dynamic_index_in_dim(gathered, source_index, 0, keepdims=False)
        down_acc = down_acc + source_term(source_row, source_index)
        down_acc = from_behind(down_acc, "row", -1)
        return (down_acc, up_acc)

    start = (jnp.zeros((ecol, beams, width), jnp.float32), jnp.zeros((1,), jnp.float32))
    far, unused_up = lax.fori_loop(0, cycle_size, step, start)
    beside = padded_2(sources, (("row", 0),), 1)
    beside = jnp.pad(beside, ((0, 0), (1, 1), (0, 0), (0, 0)))
    near = jnp.zeros((ecol * beams, width), jnp.float32)
    for index in range(near_blocks.shape[0]):
        row_offset = near_offsets[index, 0]
        col_offset = near_offsets[index, 1]
        anchor = (1 - row_offset, 1 - col_offset, jnp.int32(0), jnp.int32(0))
        shifted = lax.dynamic_slice(beside, anchor, (1, ecol, beams, width))
        near = near + jnp.dot(
            shifted.reshape(-1, width), near_blocks[index], preferred_element_type=jnp.float32
        )
    return (near.reshape(ecol, beams, width) + far).reshape(1, ecol, beams, width)


def solution(mesh):
    placed = (
        P(("grp", "row"), None, None, None),
        P(("grp", "row"), None, None, None),
        P(("grp", "row"), None, None, None),
        P(("grp", "row"), None),
        P("grp", None, None),
        P("grp", None),
    )
    return jax.shard_map(
        local,
        mesh=mesh,
        in_specs=placed,
        out_specs=P(("grp", "row"), None, None, None),
        check_vma=False,
    )
```

profile of v0, /device:TPU:0, one launch (start us, length us, event | category | flops | bytes accessed | tf_op | source)
XLA Modules:
  0.0 249.0 jit_solution(835424933795626141)
XLA Ops:
  29.0 24.7 %all-gather.2.cloned.1.call-done = bf16[16,8,8,1024]{3,2,1,0:T(8,128)(2,1)} async-done(((bf16[1,8,8,1024]{3,2,1,0:T(8,128)(2,1)}), bf16[16,8,8,1024]{3,2,1,0:T(8,128)(2,1)}) %all-gather.2.cloned.1.call-update) | async-done | bytes 2097168 | tf_op jit(solution)/shard_map/all_gather | solution.py:67
  53.7 185.6 %while.15 = (s32[]{:T(128)}, f32[8,8,1024]{2,1,0:T(8,128)S(1)}, s32[]{:T(128)}, bf16[2,15,48,1024]{3,2,1,0:T(8,128)(2,1)}, bf16[16,8,8,1024]{3,2,1,0:T(8,128)(2,...) while((s32[]{:T(128)}, f32[8,8,1024]{2,1,0:T(8,128)S(1)}, ...), condition=%wide.region_3.4_spmd, body=%wide.region_2.3_spmd.sunk | while | flops 188901376 | bytes 8549533 | solution.py:77
  59.0 3.9 %collective-permute-done = f32[8,8,1024]{2,1,0:T(8,128)S(1)} collective-permute-done((f32[8,8,1024]{2,1,0:T(8,128)S(1)}, f32[8,8,1024]{2,1,0:T(8,128)S(1)}, u32[]{:S(2)}, u32[]{:S(2)}) %collective-permute-start) | collective-permute-done | bytes 262176 | tf_op jit(solution)/shard_map/while/body/eval_jaxpr/ppermute | solution.py:13
  66.1 4.7 %collective-permute-start = (f32[8,8,1024]{2,1,0:T(8,128)S(1)}, f32[8,8,1024]{2,1,0:T(8,128)S(1)}, u32[]{:S(2)}, u32[]{:S(2)}) collective-permute-start(f32[8,8,1024]{2,1,0:T(8,128)S(1)} %fusion.81), channel_id=1, source_target_pairs={{0,15},{1,0},{2,1},{3,2},{4,3},{5,4},{6,5},{7,6},{8,7},{9,8},{10,9... | collective-permute-start | bytes 786440 | tf_op jit(solution)/shard_map/while/body/eval_jaxpr/ppermute | solution.py:13
  70.7 3.9 %collective-permute-done = f32[8,8,1024]{2,1,0:T(8,128)S(1)} collective-permute-done((f32[8,8,1024]{2,1,0:T(8,128)S(1)}, f32[8,8,1024]{2,1,0:T(8,128)S(1)}, u32[]{:S(2)}, u32[]{:S(2)}) %collective-permute-start) | collective-permute-done | bytes 262176 | tf_op jit(solution)/shard_map/while/body/eval_jaxpr/ppermute | solution.py:13
  77.8 4.7 %collective-permute-start = (f32[8,8,1024]{2,1,0:T(8,128)S(1)}, f32[8,8,1024]{2,1,0:T(8,128)S(1)}, u32[]{:S(2)}, u32[]{:S(2)}) collective-permute-start(f32[8,8,1024]{2,1,0:T(8,128)S(1)} %fusion.81), channel_id=1, source_target_pairs={{0,15},{1,0},{2,1},{3,2},{4,3},{5,4},{6,5},{7,6},{8,7},{9,8},{10,9... | collective-permute-start | bytes 786440 | tf_op jit(solution)/shard_map/while/body/eval_jaxpr/ppermute | solution.py:13
  82.5 3.9 %collective-permute-done = f32[8,8,1024]{2,1,0:T(8,128)S(1)} collective-permute-done((f32[8,8,1024]{2,1,0:T(8,128)S(1)}, f32[8,8,1024]{2,1,0:T(8,128)S(1)}, u32[]{:S(2)}, u32[]{:S(2)}) %collective-permute-start) | collective-permute-done | bytes 262176 | tf_op jit(solution)/shard_map/while/body/eval_jaxpr/ppermute | solution.py:13
  89.6 4.7 %collective-permute-start = (f32[8,8,1024]{2,1,0:T(8,128)S(1)}, f32[8,8,1024]{2,1,0:T(8,128)S(1)}, u32[]{:S(2)}, u32[]{:S(2)}) collective-permute-start(f32[8,8,1024]{2,1,0:T(8,128)S(1)} %fusion.81), channel_id=1, source_target_pairs={{0,15},{1,0},{2,1},{3,2},{4,3},{5,4},{6,5},{7,6},{8,7},{9,8},{10,9... | collective-permute-start | bytes 786440 | tf_op jit(solution)/shard_map/while/body/eval_jaxpr/ppermute | solution.py:13
  94.2 3.9 %collective-permute-done = f32[8,8,1024]{2,1,0:T(8,128)S(1)} collective-permute-done((f32[8,8,1024]{2,1,0:T(8,128)S(1)}, f32[8,8,1024]{2,1,0:T(8,128)S(1)}, u32[]{:S(2)}, u32[]{:S(2)}) %collective-permute-start) | collective-permute-done | bytes 262176 | tf_op jit(solution)/shard_map/while/body/eval_jaxpr/ppermute | solution.py:13
  101.4 4.7 %collective-permute-start = (f32[8,8,1024]{2,1,0:T(8,128)S(1)}, f32[8,8,1024]{2,1,0:T(8,128)S(1)}, u32[]{:S(2)}, u32[]{:S(2)}) collective-permute-start(f32[8,8,1024]{2,1,0:T(8,128)S(1)} %fusion.81), channel_id=1, source_target_pairs={{0,15},{1,0},{2,1},{3,2},{4,3},{5,4},{6,5},{7,6},{8,7},{9,8},{10,9... | collective-permute-start | bytes 786440 | tf_op jit(solution)/shard_map/while/body/eval_jaxpr/ppermute | solution.py:13
  106.0 3.9 %collective-permute-done = f32[8,8,1024]{2,1,0:T(8,128)S(1)} collective-permute-done((f32[8,8,1024]{2,1,0:T(8,128)S(1)}, f32[8,8,1024]{2,1,0:T(8,128)S(1)}, u32[]{:S(2)}, u32[]{:S(2)}) %collective-permute-start) | collective-permute-done | bytes 262176 | tf_op jit(solution)/shard_map/while/body/eval_jaxpr/ppermute | solution.py:13
  113.1 4.7 %collective-permute-start = (f32[8,8,1024]{2,1,0:T(8,128)S(1)}, f32[8,8,1024]{2,1,0:T(8,128)S(1)}, u32[]{:S(2)}, u32[]{:S(2)}) collective-permute-start(f32[8,8,1024]{2,1,0:T(8,128)S(1)} %fusion.81), channel_id=1, source_target_pairs={{0,15},{1,0},{2,1},{3,2},{4,3},{5,4},{6,5},{7,6},{8,7},{9,8},{10,9... | collective-permute-start | bytes 786440 | tf_op jit(solution)/shard_map/while/body/eval_jaxpr/ppermute | solution.py:13
  124.9 4.7 %collective-permute-start = (f32[8,8,1024]{2,1,0:T(8,128)S(1)}, f32[8,8,1024]{2,1,0:T(8,128)S(1)}, u32[]{:S(2)}, u32[]{:S(2)}) collective-permute-start(f32[8,8,1024]{2,1,0:T(8,128)S(1)} %fusion.81), channel_id=1, source_target_pairs={{0,15},{1,0},{2,1},{3,2},{4,3},{5,4},{6,5},{7,6},{8,7},{9,8},{10,9... | collective-permute-start | bytes 786440 | tf_op jit(solution)/shard_map/while/body/eval_jaxpr/ppermute | solution.py:13
  136.6 4.7 %collective-permute-start = (f32[8,8,1024]{2,1,0:T(8,128)S(1)}, f32[8,8,1024]{2,1,0:T(8,128)S(1)}, u32[]{:S(2)}, u32[]{:S(2)}) collective-permute-start(f32[8,8,1024]{2,1,0:T(8,128)S(1)} %fusion.81), channel_id=1, source_target_pairs={{0,15},{1,0},{2,1},{3,2},{4,3},{5,4},{6,5},{7,6},{8,7},{9,8},{10,9... | collective-permute-start | bytes 786440 | tf_op jit(solution)/shard_map/while/body/eval_jaxpr/ppermute | solution.py:13
  148.4 4.7 %collective-permute-start = (f32[8,8,1024]{2,1,0:T(8,128)S(1)}, f32[8,8,1024]{2,1,0:T(8,128)S(1)}, u32[]{:S(2)}, u32[]{:S(2)}) collective-permute-start(f32[8,8,1024]{2,1,0:T(8,128)S(1)} %fusion.81), channel_id=1, source_target_pairs={{0,15},{1,0},{2,1},{3,2},{4,3},{5,4},{6,5},{7,6},{8,7},{9,8},{10,9... | collective-permute-start | bytes 786440 | tf_op jit(solution)/shard_map/while/body/eval_jaxpr/ppermute | solution.py:13
  160.2 4.7 %collective-permute-start = (f32[8,8,1024]{2,1,0:T(8,128)S(1)}, f32[8,8,1024]{2,1,0:T(8,128)S(1)}, u32[]{:S(2)}, u32[]{:S(2)}) collective-permute-start(f32[8,8,1024]{2,1,0:T(8,128)S(1)} %fusion.81), channel_id=1, source_target_pairs={{0,15},{1,0},{2,1},{3,2},{4,3},{5,4},{6,5},{7,6},{8,7},{9,8},{10,9... | collective-permute-start | bytes 786440 | tf_op jit(solution)/shard_map/while/body/eval_jaxpr/ppermute | solution.py:13
  171.9 4.7 %collective-permute-start = (f32[8,8,1024]{2,1,0:T(8,128)S(1)}, f32[8,8,1024]{2,1,0:T(8,128)S(1)}, u32[]{:S(2)}, u32[]{:S(2)}) collective-permute-start(f32[8,8,1024]{2,1,0:T(8,128)S(1)} %fusion.81), channel_id=1, source_target_pairs={{0,15},{1,0},{2,1},{3,2},{4,3},{5,4},{6,5},{7,6},{8,7},{9,8},{10,9... | collective-permute-start | bytes 786440 | tf_op jit(solution)/shard_map/while/body/eval_jaxpr/ppermute | solution.py:13
  183.7 4.7 %collective-permute-start = (f32[8,8,1024]{2,1,0:T(8,128)S(1)}, f32[8,8,1024]{2,1,0:T(8,128)S(1)}, u32[]{:S(2)}, u32[]{:S(2)}) collective-permute-start(f32[8,8,1024]{2,1,0:T(8,128)S(1)} %fusion.81), channel_id=1, source_target_pairs={{0,15},{1,0},{2,1},{3,2},{4,3},{5,4},{6,5},{7,6},{8,7},{9,8},{10,9... | collective-permute-start | bytes 786440 | tf_op jit(solution)/shard_map/while/body/eval_jaxpr/ppermute | solution.py:13
  195.5 4.7 %collective-permute-start = (f32[8,8,1024]{2,1,0:T(8,128)S(1)}, f32[8,8,1024]{2,1,0:T(8,128)S(1)}, u32[]{:S(2)}, u32[]{:S(2)}) collective-permute-start(f32[8,8,1024]{2,1,0:T(8,128)S(1)} %fusion.81), channel_id=1, source_target_pairs={{0,15},{1,0},{2,1},{3,2},{4,3},{5,4},{6,5},{7,6},{8,7},{9,8},{10,9... | collective-permute-start | bytes 786440 | tf_op jit(solution)/shard_map/while/body/eval_jaxpr/ppermute | solution.py:13
  200.1 3.9 %collective-permute-done = f32[8,8,1024]{2,1,0:T(8,128)S(1)} collective-permute-done((f32[8,8,1024]{2,1,0:T(8,128)S(1)}, f32[8,8,1024]{2,1,0:T(8,128)S(1)}, u32[]{:S(2)}, u32[]{:S(2)}) %collective-permute-start) | collective-permute-done | bytes 262176 | tf_op jit(solution)/shard_map/while/body/eval_jaxpr/ppermute | solution.py:13
  207.2 4.7 %collective-permute-start = (f32[8,8,1024]{2,1,0:T(8,128)S(1)}, f32[8,8,1024]{2,1,0:T(8,128)S(1)}, u32[]{:S(2)}, u32[]{:S(2)}) collective-permute-start(f32[8,8,1024]{2,1,0:T(8,128)S(1)} %fusion.81), channel_id=1, source_target_pairs={{0,15},{1,0},{2,1},{3,2},{4,3},{5,4},{6,5},{7,6},{8,7},{9,8},{10,9... | collective-permute-start | bytes 786440 | tf_op jit(solution)/shard_map/while/body/eval_jaxpr/ppermute | solution.py:13
  219.0 4.7 %collective-permute-start = (f32[8,8,1024]{2,1,0:T(8,128)S(1)}, f32[8,8,1024]{2,1,0:T(8,128)S(1)}, u32[]{:S(2)}, u32[]{:S(2)}) collective-permute-start(f32[8,8,1024]{2,1,0:T(8,128)S(1)} %fusion.81), channel_id=1, source_target_pairs={{0,15},{1,0},{2,1},{3,2},{4,3},{5,4},{6,5},{7,6},{8,7},{9,8},{10,9... | collective-permute-start | bytes 786440 | tf_op jit(solution)/shard_map/while/body/eval_jaxpr/ppermute | solution.py:13
  223.7 3.9 %collective-permute-done = f32[8,8,1024]{2,1,0:T(8,128)S(1)} collective-permute-done((f32[8,8,1024]{2,1,0:T(8,128)S(1)}, f32[8,8,1024]{2,1,0:T(8,128)S(1)}, u32[]{:S(2)}, u32[]{:S(2)}) %collective-permute-start) | collective-permute-done | bytes 262176 | tf_op jit(solution)/shard_map/while/body/eval_jaxpr/ppermute | solution.py:13
  230.8 4.7 %collective-permute-start = (f32[8,8,1024]{2,1,0:T(8,128)S(1)}, f32[8,8,1024]{2,1,0:T(8,128)S(1)}, u32[]{:S(2)}, u32[]{:S(2)}) collective-permute-start(f32[8,8,1024]{2,1,0:T(8,128)S(1)} %fusion.81), channel_id=1, source_target_pairs={{0,15},{1,0},{2,1},{3,2},{4,3},{5,4},{6,5},{7,6},{8,7},{9,8},{10,9... | collective-permute-start | bytes 786440 | tf_op jit(solution)/shard_map/while/body/eval_jaxpr/ppermute | solution.py:13
  (323 shorter events, 105.3 us)
Async XLA Ops:
  6.5 47.1 %all-gather.2.cloned.1.call-start = ((), (), s32[]{:S(2)}) async-start(), calls=%async_computation | async-start | bytes 2228224 | tf_op jit(solution)/shard_map/all_gather | solution.py:67
  7.3 14.9 %collective-permute-start.1 = (bf16[1,8,8,1024]{3,2,1,0:T(8,128)(2,1)}, bf16[1,8,8,1024]{3,2,1,0:T(8,128)(2,1)S(1)}, u32[]{:S(2)}, u32[]{:S(2)}) collective-permute-start(bf16[1,8,8,1024]{3,2,1,0:T(8,128)(2,1)} %param.8), channel_id=1, source_target_pairs={{0,1},{1,2},{2,3},{3,4},{4,5},{5,6},{6,7},{7,8},{8,9},{9,10},{10,1... | collective-permute-start | bytes 393224 | tf_op jit(solution)/shard_map/ppermute | solution.py:21
  9.6 12.5 %collective-permute-start.2 = (bf16[1,8,8,1024]{3,2,1,0:T(8,128)(2,1)}, bf16[1,8,8,1024]{3,2,1,0:T(8,128)(2,1)S(1)}, u32[]{:S(2)}, u32[]{:S(2)}) collective-permute-start(bf16[1,8,8,1024]{3,2,1,0:T(8,128)(2,1)} %param.8), channel_id=1, source_target_pairs={{1,0},{2,1},{3,2},{4,3},{5,4},{6,5},{7,6},{8,7},{9,8},{10,9},{11,1... | collective-permute-start | bytes 393224 | tf_op jit(solution)/shard_map/ppermute | solution.py:24
  22.1 31.6 %copy-start = (bf16[2,15,48,1024]{3,2,1,0:T(8,128)(2,1)S(1)}, bf16[2,15,48,1024]{3,2,1,0:T(8,128)(2,1)}, u32[]{:S(2)}) copy-start(bf16[2,15,48,1024]{3,2,1,0:T(8,128)(2,1)} %param.10) | copy-start | bytes 8847364
  23.3 3.0 %copy-start.1 = (bf16[3,10,8,1024]{3,2,1,0:T(8,128)(2,1)}, bf16[3,10,8,1024]{3,2,1,0:T(8,128)(2,1)S(1)}, u32[]{:S(2)}) copy-start(bf16[3,10,8,1024]{3,2,1,0:T(8,128)(2,1)S(1)} %fusion.54) | copy-start | bytes 1474564
  57.0 5.9 %collective-permute-start = (f32[8,8,1024]{2,1,0:T(8,128)S(1)}, f32[8,8,1024]{2,1,0:T(8,128)S(1)}, u32[]{:S(2)}, u32[]{:S(2)}) collective-permute-start(f32[8,8,1024]{2,1,0:T(8,128)S(1)} %fusion.81), channel_id=1, source_target_pairs={{0,15},{1,0},{2,1},{3,2},{4,3},{5,4},{6,5},{7,6},{8,7},{9,8},{10,9... | collective-permute-start | bytes 786440 | tf_op jit(solution)/shard_map/while/body/eval_jaxpr/ppermute | solution.py:13
  66.1 8.5 %collective-permute-start = (f32[8,8,1024]{2,1,0:T(8,128)S(1)}, f32[8,8,1024]{2,1,0:T(8,128)S(1)}, u32[]{:S(2)}, u32[]{:S(2)}) collective-permute-start(f32[8,8,1024]{2,1,0:T(8,128)S(1)} %fusion.81), channel_id=1, source_target_pairs={{0,15},{1,0},{2,1},{3,2},{4,3},{5,4},{6,5},{7,6},{8,7},{9,8},{10,9... | collective-permute-start | bytes 786440 | tf_op jit(solution)/shard_map/while/body/eval_jaxpr/ppermute | solution.py:13
  77.8 8.5 %collective-permute-start = (f32[8,8,1024]{2,1,0:T(8,128)S(1)}, f32[8,8,1024]{2,1,0:T(8,128)S(1)}, u32[]{:S(2)}, u32[]{:S(2)}) collective-permute-start(f32[8,8,1024]{2,1,0:T(8,128)S(1)} %fusion.81), channel_id=1, source_target_pairs={{0,15},{1,0},{2,1},{3,2},{4,3},{5,4},{6,5},{7,6},{8,7},{9,8},{10,9... | collective-permute-start | bytes 786440 | tf_op jit(solution)/shard_map/while/body/eval_jaxpr/ppermute | solution.py:13
  89.6 8.5 %collective-permute-start = (f32[8,8,1024]{2,1,0:T(8,128)S(1)}, f32[8,8,1024]{2,1,0:T(8,128)S(1)}, u32[]{:S(2)}, u32[]{:S(2)}) collective-permute-start(f32[8,8,1024]{2,1,0:T(8,128)S(1)} %fusion.81), channel_id=1, source_target_pairs={{0,15},{1,0},{2,1},{3,2},{4,3},{5,4},{6,5},{7,6},{8,7},{9,8},{10,9... | collective-permute-start | bytes 786440 | tf_op jit(solution)/shard_map/while/body/eval_jaxpr/ppermute | solution.py:13
  101.4 8.5 %collective-permute-start = (f32[8,8,1024]{2,1,0:T(8,128)S(1)}, f32[8,8,1024]{2,1,0:T(8,128)S(1)}, u32[]{:S(2)}, u32[]{:S(2)}) collective-permute-start(f32[8,8,1024]{2,1,0:T(8,128)S(1)} %fusion.81), channel_id=1, source_target_pairs={{0,15},{1,0},{2,1},{3,2},{4,3},{5,4},{6,5},{7,6},{8,7},{9,8},{10,9... | collective-permute-start | bytes 786440 | tf_op jit(solution)/shard_map/while/body/eval_jaxpr/ppermute | solution.py:13
  113.1 8.5 %collective-permute-start = (f32[8,8,1024]{2,1,0:T(8,128)S(1)}, f32[8,8,1024]{2,1,0:T(8,128)S(1)}, u32[]{:S(2)}, u32[]{:S(2)}) collective-permute-start(f32[8,8,1024]{2,1,0:T(8,128)S(1)} %fusion.81), channel_id=1, source_target_pairs={{0,15},{1,0},{2,1},{3,2},{4,3},{5,4},{6,5},{7,6},{8,7},{9,8},{10,9... | collective-permute-start | bytes 786440 | tf_op jit(solution)/shard_map/while/body/eval_jaxpr/ppermute | solution.py:13
  124.9 8.5 %collective-permute-start = (f32[8,8,1024]{2,1,0:T(8,128)S(1)}, f32[8,8,1024]{2,1,0:T(8,128)S(1)}, u32[]{:S(2)}, u32[]{:S(2)}) collective-permute-start(f32[8,8,1024]{2,1,0:T(8,128)S(1)} %fusion.81), channel_id=1, source_target_pairs={{0,15},{1,0},{2,1},{3,2},{4,3},{5,4},{6,5},{7,6},{8,7},{9,8},{10,9... | collective-permute-start | bytes 786440 | tf_op jit(solution)/shard_map/while/body/eval_jaxpr/ppermute | solution.py:13
  136.6 8.5 %collective-permute-start = (f32[8,8,1024]{2,1,0:T(8,128)S(1)}, f32[8,8,1024]{2,1,0:T(8,128)S(1)}, u32[]{:S(2)}, u32[]{:S(2)}) collective-permute-start(f32[8,8,1024]{2,1,0:T(8,128)S(1)} %fusion.81), channel_id=1, source_target_pairs={{0,15},{1,0},{2,1},{3,2},{4,3},{5,4},{6,5},{7,6},{8,7},{9,8},{10,9... | collective-permute-start | bytes 786440 | tf_op jit(solution)/shard_map/while/body/eval_jaxpr/ppermute | solution.py:13
  148.4 8.5 %collective-permute-start = (f32[8,8,1024]{2,1,0:T(8,128)S(1)}, f32[8,8,1024]{2,1,0:T(8,128)S(1)}, u32[]{:S(2)}, u32[]{:S(2)}) collective-permute-start(f32[8,8,1024]{2,1,0:T(8,128)S(1)} %fusion.81), channel_id=1, source_target_pairs={{0,15},{1,0},{2,1},{3,2},{4,3},{5,4},{6,5},{7,6},{8,7},{9,8},{10,9... | collective-permute-start | bytes 786440 | tf_op jit(solution)/shard_map/while/body/eval_jaxpr/ppermute | solution.py:13
  160.2 8.5 %collective-permute-start = (f32[8,8,1024]{2,1,0:T(8,128)S(1)}, f32[8,8,1024]{2,1,0:T(8,128)S(1)}, u32[]{:S(2)}, u32[]{:S(2)}) collective-permute-start(f32[8,8,1024]{2,1,0:T(8,128)S(1)} %fusion.81), channel_id=1, source_target_pairs={{0,15},{1,0},{2,1},{3,2},{4,3},{5,4},{6,5},{7,6},{8,7},{9,8},{10,9... | collective-permute-start | bytes 786440 | tf_op jit(solution)/shard_map/while/body/eval_jaxpr/ppermute | solution.py:13
  171.9 8.5 %collective-permute-start = (f32[8,8,1024]{2,1,0:T(8,128)S(1)}, f32[8,8,1024]{2,1,0:T(8,128)S(1)}, u32[]{:S(2)}, u32[]{:S(2)}) collective-permute-start(f32[8,8,1024]{2,1,0:T(8,128)S(1)} %fusion.81), channel_id=1, source_target_pairs={{0,15},{1,0},{2,1},{3,2},{4,3},{5,4},{6,5},{7,6},{8,7},{9,8},{10,9... | collective-permute-start | bytes 786440 | tf_op jit(solution)/shard_map/while/body/eval_jaxpr/ppermute | solution.py:13
  183.7 8.5 %collective-permute-start = (f32[8,8,1024]{2,1,0:T(8,128)S(1)}, f32[8,8,1024]{2,1,0:T(8,128)S(1)}, u32[]{:S(2)}, u32[]{:S(2)}) collective-permute-start(f32[8,8,1024]{2,1,0:T(8,128)S(1)} %fusion.81), channel_id=1, source_target_pairs={{0,15},{1,0},{2,1},{3,2},{4,3},{5,4},{6,5},{7,6},{8,7},{9,8},{10,9... | collective-permute-start | bytes 786440 | tf_op jit(solution)/shard_map/while/body/eval_jaxpr/ppermute | solution.py:13
  195.5 8.5 %collective-permute-start = (f32[8,8,1024]{2,1,0:T(8,128)S(1)}, f32[8,8,1024]{2,1,0:T(8,128)S(1)}, u32[]{:S(2)}, u32[]{:S(2)}) collective-permute-start(f32[8,8,1024]{2,1,0:T(8,128)S(1)} %fusion.81), channel_id=1, source_target_pairs={{0,15},{1,0},{2,1},{3,2},{4,3},{5,4},{6,5},{7,6},{8,7},{9,8},{10,9... | collective-permute-start | bytes 786440 | tf_op jit(solution)/shard_map/while/body/eval_jaxpr/ppermute | solution.py:13
  207.2 8.5 %collective-permute-start = (f32[8,8,1024]{2,1,0:T(8,128)S(1)}, f32[8,8,1024]{2,1,0:T(8,128)S(1)}, u32[]{:S(2)}, u32[]{:S(2)}) collective-permute-start(f32[8,8,1024]{2,1,0:T(8,128)S(1)} %fusion.81), channel_id=1, source_target_pairs={{0,15},{1,0},{2,1},{3,2},{4,3},{5,4},{6,5},{7,6},{8,7},{9,8},{10,9... | collective-permute-start | bytes 786440 | tf_op jit(solution)/shard_map/while/body/eval_jaxpr/ppermute | solution.py:13
  219.0 8.5 %collective-permute-start = (f32[8,8,1024]{2,1,0:T(8,128)S(1)}, f32[8,8,1024]{2,1,0:T(8,128)S(1)}, u32[]{:S(2)}, u32[]{:S(2)}) collective-permute-start(f32[8,8,1024]{2,1,0:T(8,128)S(1)} %fusion.81), channel_id=1, source_target_pairs={{0,15},{1,0},{2,1},{3,2},{4,3},{5,4},{6,5},{7,6},{8,7},{9,8},{10,9... | collective-permute-start | bytes 786440 | tf_op jit(solution)/shard_map/while/body/eval_jaxpr/ppermute | solution.py:13
  230.8 8.5 %collective-permute-start = (f32[8,8,1024]{2,1,0:T(8,128)S(1)}, f32[8,8,1024]{2,1,0:T(8,128)S(1)}, u32[]{:S(2)}, u32[]{:S(2)}) collective-permute-start(f32[8,8,1024]{2,1,0:T(8,128)S(1)} %fusion.81), channel_id=1, source_target_pairs={{0,15},{1,0},{2,1},{3,2},{4,3},{5,4},{6,5},{7,6},{8,7},{9,8},{10,9... | collective-permute-start | bytes 786440 | tf_op jit(solution)/shard_map/while/body/eval_jaxpr/ppermute | solution.py:13
Sparse Core Ops, SparseCore 0:
  9.5 44.1 all-gather.1
where the time goes:
time: 250 us; the launch traced here: 249 us
  waiting for transfers between devices  87.6 us (35%)
  starting transfers between devices  75.5 us (30%)
  matrix products  55.8 us (22%)
  between operations  20.8 us (8%)
  local copies, waits for them, and re-layouts  6.14 us (2%)
    ppermute x16, starting transfers between devices, from_behind(): lax.ppermute(value, axis, [(i, (i + by) % count) for i in range(count)])  71.9 us
    ppermute x16, waiting for transfers between devices, from_behind(): lax.ppermute(value, axis, [(i, (i + by) % count) for i in range(count)])  62.2 us
    dot_general x16, matrix products, far_term(): jnp.einsum('sbn,krn->skbr', source_row, left, preferred_element_type=jnp....  37.4 us
    all_gather x1, waiting for transfers between devices, local(): gathered = lax.all_gather(sources, 'row', axis=0, tiled=True)  24.7 us
    dot_general x16, matrix products, far_term(): jnp.einsum('jkbr,krn->jbn', spread(coeffs), right, preferred_element_type...  9.73 us
    dot_general x3, matrix products, local(): jnp.dot(shifted.reshape(-1, width), near_blocks[index], preferred_element...  8.65 us
  transfers between devices with their start and end apart: 19, of which 17 were waited for; matrix products, arithmetic and copies ran while one was open for 4% of the time, Pallas kernels for 0%

commit v1 on v0

--- a/solution.py
+++ b/solution.py
@@ -64,7 +64,36 @@
         keep = lax.dynamic_index_in_dim(keep_all, wrap_bit, 0, keepdims=False)
         return far_term(source_row, left, right, keep)
 
-    gathered = lax.all_gather(sources, "row", axis=0, tiled=True)
+    u1, small, after = (lax.axis_size("row"), lax.axis_index("row"), sources.shape[0])
+    made = []
+    for it, dev in enumerate(sources.shape):
+        made.append(dev * u1 if it == 0 else dev)
+    gathered = lax.dynamic_update_slice_in_dim(
+        jnp.zeros(made, sources.dtype), sources, small * after, axis=0
+    )
+    b_next = outcome_arr = sources
+    u = 1
+    while u < u1 // 2 + 1:
+        rack = []
+        it = 0
+        while it < u1:
+            rack.append((it, (it + 1) % u1))
+            it = it + 1
+        b_next = lax.ppermute(b_next, "row", perm=rack)
+        gathered = lax.dynamic_update_slice_in_dim(
+            gathered, b_next, (small - u) % u1 * after, axis=0
+        )
+        if 2 * u < u1:
+            views = []
+            it = 0
+            while it < u1:
+                views.append((it, (it - 1) % u1))
+                it = it + 1
+            outcome_arr = lax.ppermute(outcome_arr, "row", views)
+            gathered = lax.dynamic_update_slice_in_dim(
+                gathered, outcome_arr, (small + u) % u1 * after, axis=0
+            )
+        u += 1
 
     def step(source_index, accums):
         down_acc, up_acc = accums

time: 250 us -> 263 us (1.052)
  starting transfers between devices: 75.5 us -> 106 us
  between operations: 20.8 us -> 7.95 us
  waiting for transfers between devices: 87.6 us -> 81.7 us
  local copies, waits for them, and re-layouts: 6.14 us -> 8.8 us
    ppermute x0 -> x15, starting transfers between devices: none -> 33.2 us  [the longest x7 31.5 us: local(): outcome_arr = lax.ppermute(outcome_arr, 'row', views)]
    all_gather x1 -> x0, waiting for transfers between devices: 24.7 us -> none  [local(): gathered = lax.all_gather(sources, 'row', axis=0, tiled=True)]
    ppermute x0 -> x15, waiting for transfers between devices: none -> 19.5 us  [the longest x8 10.5 us: local(): b_next = lax.ppermute(b_next, 'row', perm=rack)]
  transfers between devices with their start and end apart: 19 -> 33, of which waited for: 17 -> 28; matrix products, arithmetic and copies ran while one was open for 4% -> 5% of each run, Pallas kernels for 0% -> 0%
where the time goes in v1:
time: 263 us; the launch traced here: 262 us
  starting transfers between devices  106 us (40%)
  waiting for transfers between devices  81.7 us (31%)
  matrix products  54.1 us (21%)
  local copies, waits for them, and re-layouts  8.8 us (3%)
  between operations  7.95 us (3%)
    ppermute x16, starting transfers between devices, from_behind(): lax.ppermute(value, axis, [(i, (i + by) % count) for i in range(count)])  69.9 us
    ppermute x16, waiting for transfers between devices, from_behind(): lax.ppermute(value, axis, [(i, (i + by) % count) for i in range(count)])  62.2 us
    dot_general x16, matrix products, far_term(): jnp.einsum('sbn,krn->skbr', source_row, left, preferred_element_type=jnp....  37.4 us
    ppermute x7, starting transfers between devices, local(): outcome_arr = lax.ppermute(outcome_arr, 'row', views)  31.5 us
    ppermute x8, waiting for transfers between devices, local(): b_next = lax.ppermute(b_next, 'row', perm=rack)  10.5 us
    dot_general x16, matrix products, far_term(): jnp.einsum('jkbr,krn->jbn', spread(coeffs), right, preferred_element_type...  9.75 us
    ppermute x7, waiting for transfers between devices, local(): outcome_arr = lax.ppermute(outcome_arr, 'row', views)  9 us
    dot_general x3, matrix products, local(): jnp.dot(shifted.reshape(-1, width), near_blocks[index], preferred_element...  6.92 us
  transfers between devices with their start and end apart: 33, of which 28 were waited for; matrix products, arithmetic and copies ran while one was open for 5% of the time, Pallas kernels for 0%

profile of v1, /device:TPU:0, one launch (start us, length us, event | category | flops | bytes accessed | tf_op | source)
XLA Modules:
  0.0 262.0 jit_solution(9330645696975670146)
XLA Ops:
  0.5 5.0 %collective-permute-start.4 = (bf16[1,8,8,1024]{3,2,1,0:T(8,128)(2,1)}, bf16[1,8,8,1024]{3,2,1,0:T(8,128)(2,1)S(1)}, u32[]{:S(2)}, u32[]{:S(2)}) collective-permute-start(bf16[1,8,8,1024]{3,2,1,0:T(8,128)(2,1)} %param.8), channel_id=1, source_target_pairs={{0,15},{1,0},{2,1},{3,2},{4,3},{5,4},{6,5},{7,6},{8,7},{9,8},{10,9... | collective-permute-start | bytes 393224 | tf_op jit(solution)/shard_map/ppermute | solution.py:92
  34.0 4.7 %collective-permute-start.8 = (bf16[1,8,8,1024]{3,2,1,0:T(8,128)(2,1)S(1)}, bf16[1,8,8,1024]{3,2,1,0:T(8,128)(2,1)S(1)}, u32[]{:S(2)}, u32[]{:S(2)}) collective-permute-start(bf16[1,8,8,1024]{3,2,1,0:T(8,128)(2,1)S(1)} %collective-permute-done.6), channel_id=1, source_target_pairs={{0,15},{1,0},{2,1},{3,2},{4,3},{5,4},{6,5},{7,6},{8,7},{9,8},{10,9... | collective-permute-start | bytes 393224 | tf_op jit(solution)/shard_map/ppermute | solution.py:92
  41.2 4.6 %collective-permute-start.10 = (bf16[1,8,8,1024]{3,2,1,0:T(8,128)(2,1)S(1)}, bf16[1,8,8,1024]{3,2,1,0:T(8,128)(2,1)S(1)}, u32[]{:S(2)}, u32[]{:S(2)}) collective-permute-start(bf16[1,8,8,1024]{3,2,1,0:T(8,128)(2,1)S(1)} %collective-permute-done.8), channel_id=1, source_target_pairs={{0,15},{1,0},{2,1},{3,2},{4,3},{5,4},{6,5},{7,6},{8,7},{9,8},{10,9... | collective-permute-start | bytes 393224 | tf_op jit(solution)/shard_map/ppermute | solution.py:92
  48.3 4.6 %collective-permute-start.12 = (bf16[1,8,8,1024]{3,2,1,0:T(8,128)(2,1)S(1)}, bf16[1,8,8,1024]{3,2,1,0:T(8,128)(2,1)S(1)}, u32[]{:S(2)}, u32[]{:S(2)}) collective-permute-start(bf16[1,8,8,1024]{3,2,1,0:T(8,128)(2,1)S(1)} %collective-permute-done.10), channel_id=1, source_target_pairs={{0,15},{1,0},{2,1},{3,2},{4,3},{5,4},{6,5},{7,6},{8,7},{9,8},{10,9... | collective-permute-start | bytes 393224 | tf_op jit(solution)/shard_map/ppermute | solution.py:92
  55.5 4.7 %collective-permute-start.14 = (bf16[1,8,8,1024]{3,2,1,0:T(8,128)(2,1)S(1)}, bf16[1,8,8,1024]{3,2,1,0:T(8,128)(2,1)S(1)}, u32[]{:S(2)}, u32[]{:S(2)}) collective-permute-start(bf16[1,8,8,1024]{3,2,1,0:T(8,128)(2,1)S(1)} %collective-permute-done.12), channel_id=1, source_target_pairs={{0,15},{1,0},{2,1},{3,2},{4,3},{5,4},{6,5},{7,6},{8,7},{9,8},{10,9... | collective-permute-start | bytes 393224 | tf_op jit(solution)/shard_map/ppermute | solution.py:92
  62.7 4.6 %collective-permute-start.16 = (bf16[1,8,8,1024]{3,2,1,0:T(8,128)(2,1)S(1)}, bf16[1,8,8,1024]{3,2,1,0:T(8,128)(2,1)S(1)}, u32[]{:S(2)}, u32[]{:S(2)}) collective-permute-start(bf16[1,8,8,1024]{3,2,1,0:T(8,128)(2,1)S(1)} %collective-permute-done.14), channel_id=1, source_target_pairs={{0,15},{1,0},{2,1},{3,2},{4,3},{5,4},{6,5},{7,6},{8,7},{9,8},{10,9... | collective-permute-start | bytes 393224 | tf_op jit(solution)/shard_map/ppermute | solution.py:92
  69.8 5.6 %collective-permute-done.17 = bf16[1,8,8,1024]{3,2,1,0:T(8,128)(2,1)S(1)} collective-permute-done((bf16[1,8,8,1024]{3,2,1,0:T(8,128)(2,1)S(1)}, bf16[1,8,8,1024]{3,2,1,0:T(8,128)(2,1)S(1)}, u32[]{:S(2)}, u32[]{:S(2)}) %collective-permute-start.17) | collective-permute-done | bytes 131104 | tf_op jit(solution)/shard_map/ppermute | solution.py:82
  76.7 183.6 %while.15 = (s32[]{:T(128)}, f32[8,8,1024]{2,1,0:T(8,128)S(1)}, s32[]{:T(128)}, bf16[2,15,48,1024]{3,2,1,0:T(8,128)(2,1)}, bf16[16,8,8,1024]{3,2,1,0:T(8,128)(2,...) while((s32[]{:T(128)}, f32[8,8,1024]{2,1,0:T(8,128)S(1)}, ...), condition=%wide.region_3.4_spmd, body=%wide.region_2.3_spmd.sunk | while | flops 188901376 | bytes 8549533 | solution.py:106
  87.1 4.7 %collective-permute-start = (f32[8,8,1024]{2,1,0:T(8,128)S(1)}, f32[8,8,1024]{2,1,0:T(8,128)S(1)}, u32[]{:S(2)}, u32[]{:S(2)}) collective-permute-start(f32[8,8,1024]{2,1,0:T(8,128)S(1)} %fusion.75), channel_id=1, source_target_pairs={{0,15},{1,0},{2,1},{3,2},{4,3},{5,4},{6,5},{7,6},{8,7},{9,8},{10,9... | collective-permute-start | bytes 786440 | tf_op jit(solution)/shard_map/while/body/eval_jaxpr/ppermute | solution.py:13
  91.8 3.9 %collective-permute-done = f32[8,8,1024]{2,1,0:T(8,128)S(1)} collective-permute-done((f32[8,8,1024]{2,1,0:T(8,128)S(1)}, f32[8,8,1024]{2,1,0:T(8,128)S(1)}, u32[]{:S(2)}, u32[]{:S(2)}) %collective-permute-start) | collective-permute-done | bytes 262176 | tf_op jit(solution)/shard_map/while/body/eval_jaxpr/ppermute | solution.py:13
  98.9 4.7 %collective-permute-start = (f32[8,8,1024]{2,1,0:T(8,128)S(1)}, f32[8,8,1024]{2,1,0:T(8,128)S(1)}, u32[]{:S(2)}, u32[]{:S(2)}) collective-permute-start(f32[8,8,1024]{2,1,0:T(8,128)S(1)} %fusion.75), channel_id=1, source_target_pairs={{0,15},{1,0},{2,1},{3,2},{4,3},{5,4},{6,5},{7,6},{8,7},{9,8},{10,9... | collective-permute-start | bytes 786440 | tf_op jit(solution)/shard_map/while/body/eval_jaxpr/ppermute | solution.py:13
  110.6 4.7 %collective-permute-start = (f32[8,8,1024]{2,1,0:T(8,128)S(1)}, f32[8,8,1024]{2,1,0:T(8,128)S(1)}, u32[]{:S(2)}, u32[]{:S(2)}) collective-permute-start(f32[8,8,1024]{2,1,0:T(8,128)S(1)} %fusion.75), channel_id=1, source_target_pairs={{0,15},{1,0},{2,1},{3,2},{4,3},{5,4},{6,5},{7,6},{8,7},{9,8},{10,9... | collective-permute-start | bytes 786440 | tf_op jit(solution)/shard_map/while/body/eval_jaxpr/ppermute | solution.py:13
  122.4 4.7 %collective-permute-start = (f32[8,8,1024]{2,1,0:T(8,128)S(1)}, f32[8,8,1024]{2,1,0:T(8,128)S(1)}, u32[]{:S(2)}, u32[]{:S(2)}) collective-permute-start(f32[8,8,1024]{2,1,0:T(8,128)S(1)} %fusion.75), channel_id=1, source_target_pairs={{0,15},{1,0},{2,1},{3,2},{4,3},{5,4},{6,5},{7,6},{8,7},{9,8},{10,9... | collective-permute-start | bytes 786440 | tf_op jit(solution)/shard_map/while/body/eval_jaxpr/ppermute | solution.py:13
  134.2 4.7 %collective-permute-start = (f32[8,8,1024]{2,1,0:T(8,128)S(1)}, f32[8,8,1024]{2,1,0:T(8,128)S(1)}, u32[]{:S(2)}, u32[]{:S(2)}) collective-permute-start(f32[8,8,1024]{2,1,0:T(8,128)S(1)} %fusion.75), channel_id=1, source_target_pairs={{0,15},{1,0},{2,1},{3,2},{4,3},{5,4},{6,5},{7,6},{8,7},{9,8},{10,9... | collective-permute-start | bytes 786440 | tf_op jit(solution)/shard_map/while/body/eval_jaxpr/ppermute | solution.py:13
  145.9 4.7 %collective-permute-start = (f32[8,8,1024]{2,1,0:T(8,128)S(1)}, f32[8,8,1024]{2,1,0:T(8,128)S(1)}, u32[]{:S(2)}, u32[]{:S(2)}) collective-permute-start(f32[8,8,1024]{2,1,0:T(8,128)S(1)} %fusion.75), channel_id=1, source_target_pairs={{0,15},{1,0},{2,1},{3,2},{4,3},{5,4},{6,5},{7,6},{8,7},{9,8},{10,9... | collective-permute-start | bytes 786440 | tf_op jit(solution)/shard_map/while/body/eval_jaxpr/ppermute | solution.py:13
  157.7 4.7 %collective-permute-start = (f32[8,8,1024]{2,1,0:T(8,128)S(1)}, f32[8,8,1024]{2,1,0:T(8,128)S(1)}, u32[]{:S(2)}, u32[]{:S(2)}) collective-permute-start(f32[8,8,1024]{2,1,0:T(8,128)S(1)} %fusion.75), channel_id=1, source_target_pairs={{0,15},{1,0},{2,1},{3,2},{4,3},{5,4},{6,5},{7,6},{8,7},{9,8},{10,9... | collective-permute-start | bytes 786440 | tf_op jit(solution)/shard_map/while/body/eval_jaxpr/ppermute | solution.py:13
  169.5 4.7 %collective-permute-start = (f32[8,8,1024]{2,1,0:T(8,128)S(1)}, f32[8,8,1024]{2,1,0:T(8,128)S(1)}, u32[]{:S(2)}, u32[]{:S(2)}) collective-permute-start(f32[8,8,1024]{2,1,0:T(8,128)S(1)} %fusion.75), channel_id=1, source_target_pairs={{0,15},{1,0},{2,1},{3,2},{4,3},{5,4},{6,5},{7,6},{8,7},{9,8},{10,9... | collective-permute-start | bytes 786440 | tf_op jit(solution)/shard_map/while/body/eval_jaxpr/ppermute | solution.py:13
  181.2 4.7 %collective-permute-start = (f32[8,8,1024]{2,1,0:T(8,128)S(1)}, f32[8,8,1024]{2,1,0:T(8,128)S(1)}, u32[]{:S(2)}, u32[]{:S(2)}) collective-permute-start(f32[8,8,1024]{2,1,0:T(8,128)S(1)} %fusion.75), channel_id=1, source_target_pairs={{0,15},{1,0},{2,1},{3,2},{4,3},{5,4},{6,5},{7,6},{8,7},{9,8},{10,9... | collective-permute-start | bytes 786440 | tf_op jit(solution)/shard_map/while/body/eval_jaxpr/ppermute | solution.py:13
  193.0 4.7 %collective-permute-start = (f32[8,8,1024]{2,1,0:T(8,128)S(1)}, f32[8,8,1024]{2,1,0:T(8,128)S(1)}, u32[]{:S(2)}, u32[]{:S(2)}) collective-permute-start(f32[8,8,1024]{2,1,0:T(8,128)S(1)} %fusion.75), channel_id=1, source_target_pairs={{0,15},{1,0},{2,1},{3,2},{4,3},{5,4},{6,5},{7,6},{8,7},{9,8},{10,9... | collective-permute-start | bytes 786440 | tf_op jit(solution)/shard_map/while/body/eval_jaxpr/ppermute | solution.py:13
  204.8 4.7 %collective-permute-start = (f32[8,8,1024]{2,1,0:T(8,128)S(1)}, f32[8,8,1024]{2,1,0:T(8,128)S(1)}, u32[]{:S(2)}, u32[]{:S(2)}) collective-permute-start(f32[8,8,1024]{2,1,0:T(8,128)S(1)} %fusion.75), channel_id=1, source_target_pairs={{0,15},{1,0},{2,1},{3,2},{4,3},{5,4},{6,5},{7,6},{8,7},{9,8},{10,9... | collective-permute-start | bytes 786440 | tf_op jit(solution)/shard_map/while/body/eval_jaxpr/ppermute | solution.py:13
  216.5 4.7 %collective-permute-start = (f32[8,8,1024]{2,1,0:T(8,128)S(1)}, f32[8,8,1024]{2,1,0:T(8,128)S(1)}, u32[]{:S(2)}, u32[]{:S(2)}) collective-permute-start(f32[8,8,1024]{2,1,0:T(8,128)S(1)} %fusion.75), channel_id=1, source_target_pairs={{0,15},{1,0},{2,1},{3,2},{4,3},{5,4},{6,5},{7,6},{8,7},{9,8},{10,9... | collective-permute-start | bytes 786440 | tf_op jit(solution)/shard_map/while/body/eval_jaxpr/ppermute | solution.py:13
  228.3 4.7 %collective-permute-start = (f32[8,8,1024]{2,1,0:T(8,128)S(1)}, f32[8,8,1024]{2,1,0:T(8,128)S(1)}, u32[]{:S(2)}, u32[]{:S(2)}) collective-permute-start(f32[8,8,1024]{2,1,0:T(8,128)S(1)} %fusion.75), channel_id=1, source_target_pairs={{0,15},{1,0},{2,1},{3,2},{4,3},{5,4},{6,5},{7,6},{8,7},{9,8},{10,9... | collective-permute-start | bytes 786440 | tf_op jit(solution)/shard_map/while/body/eval_jaxpr/ppermute | solution.py:13
  240.0 4.7 %collective-permute-start = (f32[8,8,1024]{2,1,0:T(8,128)S(1)}, f32[8,8,1024]{2,1,0:T(8,128)S(1)}, u32[]{:S(2)}, u32[]{:S(2)}) collective-permute-start(f32[8,8,1024]{2,1,0:T(8,128)S(1)} %fusion.75), channel_id=1, source_target_pairs={{0,15},{1,0},{2,1},{3,2},{4,3},{5,4},{6,5},{7,6},{8,7},{9,8},{10,9... | collective-permute-start | bytes 786440 | tf_op jit(solution)/shard_map/while/body/eval_jaxpr/ppermute | solution.py:13
  251.8 4.7 %collective-permute-start = (f32[8,8,1024]{2,1,0:T(8,128)S(1)}, f32[8,8,1024]{2,1,0:T(8,128)S(1)}, u32[]{:S(2)}, u32[]{:S(2)}) collective-permute-start(f32[8,8,1024]{2,1,0:T(8,128)S(1)} %fusion.75), channel_id=1, source_target_pairs={{0,15},{1,0},{2,1},{3,2},{4,3},{5,4},{6,5},{7,6},{8,7},{9,8},{10,9... | collective-permute-start | bytes 786440 | tf_op jit(solution)/shard_map/while/body/eval_jaxpr/ppermute | solution.py:13
  (370 shorter events, 145.4 us)
Async XLA Ops:
  0.0 24.2 %collective-permute-start.3 = (bf16[1,8,8,1024]{3,2,1,0:T(8,128)(2,1)}, bf16[1,8,8,1024]{3,2,1,0:T(8,128)(2,1)}, u32[]{:S(2)}, u32[]{:S(2)}) collective-permute-start(bf16[1,8,8,1024]{3,2,1,0:T(8,128)(2,1)} %param.8), channel_id=1, source_target_pairs={{0,1},{1,2},{2,3},{3,4},{4,5},{5,6},{6,7},{7,8},{8,9},{9,10},{10,1... | collective-permute-start | bytes 393224 | tf_op jit(solution)/shard_map/ppermute | solution.py:82
  0.5 27.7 %collective-permute-start.4 = (bf16[1,8,8,1024]{3,2,1,0:T(8,128)(2,1)}, bf16[1,8,8,1024]{3,2,1,0:T(8,128)(2,1)S(1)}, u32[]{:S(2)}, u32[]{:S(2)}) collective-permute-start(bf16[1,8,8,1024]{3,2,1,0:T(8,128)(2,1)} %param.8), channel_id=1, source_target_pairs={{0,15},{1,0},{2,1},{3,2},{4,3},{5,4},{6,5},{7,6},{8,7},{9,8},{10,9... | collective-permute-start | bytes 393224 | tf_op jit(solution)/shard_map/ppermute | solution.py:92
  5.5 14.5 %collective-permute-start.1 = (bf16[1,8,8,1024]{3,2,1,0:T(8,128)(2,1)}, bf16[1,8,8,1024]{3,2,1,0:T(8,128)(2,1)S(1)}, u32[]{:S(2)}, u32[]{:S(2)}) collective-permute-start(bf16[1,8,8,1024]{3,2,1,0:T(8,128)(2,1)} %param.8), channel_id=1, source_target_pairs={{0,1},{1,2},{2,3},{3,4},{4,5},{5,6},{6,7},{7,8},{8,9},{9,10},{10,1... | collective-permute-start | bytes 393224 | tf_op jit(solution)/shard_map/ppermute | solution.py:21
  6.8 13.2 %collective-permute-start.2 = (bf16[1,8,8,1024]{3,2,1,0:T(8,128)(2,1)}, bf16[1,8,8,1024]{3,2,1,0:T(8,128)(2,1)S(1)}, u32[]{:S(2)}, u32[]{:S(2)}) collective-permute-start(bf16[1,8,8,1024]{3,2,1,0:T(8,128)(2,1)} %param.8), channel_id=1, source_target_pairs={{1,0},{2,1},{3,2},{4,3},{5,4},{6,5},{7,6},{8,7},{9,8},{10,9},{11,1... | collective-permute-start | bytes 393224 | tf_op jit(solution)/shard_map/ppermute | solution.py:24
  24.2 8.2 %collective-permute-start.5 = (bf16[1,8,8,1024]{3,2,1,0:T(8,128)(2,1)}, bf16[1,8,8,1024]{3,2,1,0:T(8,128)(2,1)S(1)}, u32[]{:S(2)}, u32[]{:S(2)}) collective-permute-start(bf16[1,8,8,1024]{3,2,1,0:T(8,128)(2,1)} %collective-permute-done.3), channel_id=1, source_target_pairs={{0,1},{1,2},{2,3},{3,4},{4,5},{5,6},{6,7},{7,8},{8,9},{9,10},{10,1... | collective-permute-start | bytes 393224 | tf_op jit(solution)/shard_map/ppermute | solution.py:82
  32.5 7.2 %collective-permute-start.7 = (bf16[1,8,8,1024]{3,2,1,0:T(8,128)(2,1)S(1)}, bf16[1,8,8,1024]{3,2,1,0:T(8,128)(2,1)S(1)}, u32[]{:S(2)}, u32[]{:S(2)}) collective-permute-start(bf16[1,8,8,1024]{3,2,1,0:T(8,128)(2,1)S(1)} %collective-permute-done.5), channel_id=1, source_target_pairs={{0,1},{1,2},{2,3},{3,4},{4,5},{5,6},{6,7},{7,8},{8,9},{9,10},{10,1... | collective-permute-start | bytes 393224 | tf_op jit(solution)/shard_map/ppermute | solution.py:82
  34.0 7.2 %collective-permute-start.8 = (bf16[1,8,8,1024]{3,2,1,0:T(8,128)(2,1)S(1)}, bf16[1,8,8,1024]{3,2,1,0:T(8,128)(2,1)S(1)}, u32[]{:S(2)}, u32[]{:S(2)}) collective-permute-start(bf16[1,8,8,1024]{3,2,1,0:T(8,128)(2,1)S(1)} %collective-permute-done.6), channel_id=1, source_target_pairs={{0,15},{1,0},{2,1},{3,2},{4,3},{5,4},{6,5},{7,6},{8,7},{9,8},{10,9... | collective-permute-start | bytes 393224 | tf_op jit(solution)/shard_map/ppermute | solution.py:92
  46.8 7.2 %collective-permute-start.11 = (bf16[1,8,8,1024]{3,2,1,0:T(8,128)(2,1)S(1)}, bf16[1,8,8,1024]{3,2,1,0:T(8,128)(2,1)S(1)}, u32[]{:S(2)}, u32[]{:S(2)}) collective-permute-start(bf16[1,8,8,1024]{3,2,1,0:T(8,128)(2,1)S(1)} %collective-permute-done.9), channel_id=1, source_target_pairs={{0,1},{1,2},{2,3},{3,4},{4,5},{5,6},{6,7},{7,8},{8,9},{9,10},{10,1... | collective-permute-start | bytes 393224 | tf_op jit(solution)/shard_map/ppermute | solution.py:82
  55.5 7.2 %collective-permute-start.14 = (bf16[1,8,8,1024]{3,2,1,0:T(8,128)(2,1)S(1)}, bf16[1,8,8,1024]{3,2,1,0:T(8,128)(2,1)S(1)}, u32[]{:S(2)}, u32[]{:S(2)}) collective-permute-start(bf16[1,8,8,1024]{3,2,1,0:T(8,128)(2,1)S(1)} %collective-permute-done.12), channel_id=1, source_target_pairs={{0,15},{1,0},{2,1},{3,2},{4,3},{5,4},{6,5},{7,6},{8,7},{9,8},{10,9... | collective-permute-start | bytes 393224 | tf_op jit(solution)/shard_map/ppermute | solution.py:92
  87.1 8.5 %collective-permute-start = (f32[8,8,1024]{2,1,0:T(8,128)S(1)}, f32[8,8,1024]{2,1,0:T(8,128)S(1)}, u32[]{:S(2)}, u32[]{:S(2)}) collective-permute-start(f32[8,8,1024]{2,1,0:T(8,128)S(1)} %fusion.75), channel_id=1, source_target_pairs={{0,15},{1,0},{2,1},{3,2},{4,3},{5,4},{6,5},{7,6},{8,7},{9,8},{10,9... | collective-permute-start | bytes 786440 | tf_op jit(solution)/shard_map/while/body/eval_jaxpr/ppermute | solution.py:13
  98.9 8.5 %collective-permute-start = (f32[8,8,1024]{2,1,0:T(8,128)S(1)}, f32[8,8,1024]{2,1,0:T(8,128)S(1)}, u32[]{:S(2)}, u32[]{:S(2)}) collective-permute-start(f32[8,8,1024]{2,1,0:T(8,128)S(1)} %fusion.75), channel_id=1, source_target_pairs={{0,15},{1,0},{2,1},{3,2},{4,3},{5,4},{6,5},{7,6},{8,7},{9,8},{10,9... | collective-permute-start | bytes 786440 | tf_op jit(solution)/shard_map/while/body/eval_jaxpr/ppermute | solution.py:13
  110.6 8.5 %collective-permute-start = (f32[8,8,1024]{2,1,0:T(8,128)S(1)}, f32[8,8,1024]{2,1,0:T(8,128)S(1)}, u32[]{:S(2)}, u32[]{:S(2)}) collective-permute-start(f32[8,8,1024]{2,1,0:T(8,128)S(1)} %fusion.75), channel_id=1, source_target_pairs={{0,15},{1,0},{2,1},{3,2},{4,3},{5,4},{6,5},{7,6},{8,7},{9,8},{10,9... | collective-permute-start | bytes 786440 | tf_op jit(solution)/shard_map/while/body/eval_jaxpr/ppermute | solution.py:13
  122.4 8.6 %collective-permute-start = (f32[8,8,1024]{2,1,0:T(8,128)S(1)}, f32[8,8,1024]{2,1,0:T(8,128)S(1)}, u32[]{:S(2)}, u32[]{:S(2)}) collective-permute-start(f32[8,8,1024]{2,1,0:T(8,128)S(1)} %fusion.75), channel_id=1, source_target_pairs={{0,15},{1,0},{2,1},{3,2},{4,3},{5,4},{6,5},{7,6},{8,7},{9,8},{10,9... | collective-permute-start | bytes 786440 | tf_op jit(solution)/shard_map/while/body/eval_jaxpr/ppermute | solution.py:13
  134.2 8.5 %collective-permute-start = (f32[8,8,1024]{2,1,0:T(8,128)S(1)}, f32[8,8,1024]{2,1,0:T(8,128)S(1)}, u32[]{:S(2)}, u32[]{:S(2)}) collective-permute-start(f32[8,8,1024]{2,1,0:T(8,128)S(1)} %fusion.75), channel_id=1, source_target_pairs={{0,15},{1,0},{2,1},{3,2},{4,3},{5,4},{6,5},{7,6},{8,7},{9,8},{10,9... | collective-permute-start | bytes 786440 | tf_op jit(solution)/shard_map/while/body/eval_jaxpr/ppermute | solution.py:13
  145.9 8.6 %collective-permute-start = (f32[8,8,1024]{2,1,0:T(8,128)S(1)}, f32[8,8,1024]{2,1,0:T(8,128)S(1)}, u32[]{:S(2)}, u32[]{:S(2)}) collective-permute-start(f32[8,8,1024]{2,1,0:T(8,128)S(1)} %fusion.75), channel_id=1, source_target_pairs={{0,15},{1,0},{2,1},{3,2},{4,3},{5,4},{6,5},{7,6},{8,7},{9,8},{10,9... | collective-permute-start | bytes 786440 | tf_op jit(solution)/shard_map/while/body/eval_jaxpr/ppermute | solution.py:13
  157.7 8.5 %collective-permute-start = (f32[8,8,1024]{2,1,0:T(8,128)S(1)}, f32[8,8,1024]{2,1,0:T(8,128)S(1)}, u32[]{:S(2)}, u32[]{:S(2)}) collective-permute-start(f32[8,8,1024]{2,1,0:T(8,128)S(1)} %fusion.75), channel_id=1, source_target_pairs={{0,15},{1,0},{2,1},{3,2},{4,3},{5,4},{6,5},{7,6},{8,7},{9,8},{10,9... | collective-permute-start | bytes 786440 | tf_op jit(solution)/shard_map/while/body/eval_jaxpr/ppermute | solution.py:13
  169.5 8.6 %collective-permute-start = (f32[8,8,1024]{2,1,0:T(8,128)S(1)}, f32[8,8,1024]{2,1,0:T(8,128)S(1)}, u32[]{:S(2)}, u32[]{:S(2)}) collective-permute-start(f32[8,8,1024]{2,1,0:T(8,128)S(1)} %fusion.75), channel_id=1, source_target_pairs={{0,15},{1,0},{2,1},{3,2},{4,3},{5,4},{6,5},{7,6},{8,7},{9,8},{10,9... | collective-permute-start | bytes 786440 | tf_op jit(solution)/shard_map/while/body/eval_jaxpr/ppermute | solution.py:13
  181.2 8.5 %collective-permute-start = (f32[8,8,1024]{2,1,0:T(8,128)S(1)}, f32[8,8,1024]{2,1,0:T(8,128)S(1)}, u32[]{:S(2)}, u32[]{:S(2)}) collective-permute-start(f32[8,8,1024]{2,1,0:T(8,128)S(1)} %fusion.75), channel_id=1, source_target_pairs={{0,15},{1,0},{2,1},{3,2},{4,3},{5,4},{6,5},{7,6},{8,7},{9,8},{10,9... | collective-permute-start | bytes 786440 | tf_op jit(solution)/shard_map/while/body/eval_jaxpr/ppermute | solution.py:13
  193.0 8.6 %collective-permute-start = (f32[8,8,1024]{2,1,0:T(8,128)S(1)}, f32[8,8,1024]{2,1,0:T(8,128)S(1)}, u32[]{:S(2)}, u32[]{:S(2)}) collective-permute-start(f32[8,8,1024]{2,1,0:T(8,128)S(1)} %fusion.75), channel_id=1, source_target_pairs={{0,15},{1,0},{2,1},{3,2},{4,3},{5,4},{6,5},{7,6},{8,7},{9,8},{10,9... | collective-permute-start | bytes 786440 | tf_op jit(solution)/shard_map/while/body/eval_jaxpr/ppermute | solution.py:13
  204.8 8.5 %collective-permute-start = (f32[8,8,1024]{2,1,0:T(8,128)S(1)}, f32[8,8,1024]{2,1,0:T(8,128)S(1)}, u32[]{:S(2)}, u32[]{:S(2)}) collective-permute-start(f32[8,8,1024]{2,1,0:T(8,128)S(1)} %fusion.75), channel_id=1, source_target_pairs={{0,15},{1,0},{2,1},{3,2},{4,3},{5,4},{6,5},{7,6},{8,7},{9,8},{10,9... | collective-permute-start | bytes 786440 | tf_op jit(solution)/shard_map/while/body/eval_jaxpr/ppermute | solution.py:13
  216.5 8.6 %collective-permute-start = (f32[8,8,1024]{2,1,0:T(8,128)S(1)}, f32[8,8,1024]{2,1,0:T(8,128)S(1)}, u32[]{:S(2)}, u32[]{:S(2)}) collective-permute-start(f32[8,8,1024]{2,1,0:T(8,128)S(1)} %fusion.75), channel_id=1, source_target_pairs={{0,15},{1,0},{2,1},{3,2},{4,3},{5,4},{6,5},{7,6},{8,7},{9,8},{10,9... | collective-permute-start | bytes 786440 | tf_op jit(solution)/shard_map/while/body/eval_jaxpr/ppermute | solution.py:13
  228.3 8.5 %collective-permute-start = (f32[8,8,1024]{2,1,0:T(8,128)S(1)}, f32[8,8,1024]{2,1,0:T(8,128)S(1)}, u32[]{:S(2)}, u32[]{:S(2)}) collective-permute-start(f32[8,8,1024]{2,1,0:T(8,128)S(1)} %fusion.75), channel_id=1, source_target_pairs={{0,15},{1,0},{2,1},{3,2},{4,3},{5,4},{6,5},{7,6},{8,7},{9,8},{10,9... | collective-permute-start | bytes 786440 | tf_op jit(solution)/shard_map/while/body/eval_jaxpr/ppermute | solution.py:13
  240.0 8.6 %collective-permute-start = (f32[8,8,1024]{2,1,0:T(8,128)S(1)}, f32[8,8,1024]{2,1,0:T(8,128)S(1)}, u32[]{:S(2)}, u32[]{:S(2)}) collective-permute-start(f32[8,8,1024]{2,1,0:T(8,128)S(1)} %fusion.75), channel_id=1, source_target_pairs={{0,15},{1,0},{2,1},{3,2},{4,3},{5,4},{6,5},{7,6},{8,7},{9,8},{10,9... | collective-permute-start | bytes 786440 | tf_op jit(solution)/shard_map/while/body/eval_jaxpr/ppermute | solution.py:13
  251.8 8.5 %collective-permute-start = (f32[8,8,1024]{2,1,0:T(8,128)S(1)}, f32[8,8,1024]{2,1,0:T(8,128)S(1)}, u32[]{:S(2)}, u32[]{:S(2)}) collective-permute-start(f32[8,8,1024]{2,1,0:T(8,128)S(1)} %fusion.75), channel_id=1, source_target_pairs={{0,15},{1,0},{2,1},{3,2},{4,3},{5,4},{6,5},{7,6},{8,7},{9,8},{10,9... | collective-permute-start | bytes 786440 | tf_op jit(solution)/shard_map/while/body/eval_jaxpr/ppermute | solution.py:13
  (12 other events, 129.4 us)
